TPU v7x, 32 devices: a whole 2x2x4 slice. The times are simulated.
32 devices in a mesh: grp: 2 (over core), dp: 16 (over z, y, x).
Axes of the slice: x: 2, y: 2, z: 4, core: 2. Of those that a mesh axis runs over, the one named last changes fastest.
Arguments:
- tokens: bfloat16 [32768, 768], P(('grp', 'dp')), may hold values from -6 to 6
- out_grad: bfloat16 [32768, 768], P(('grp', 'dp')), may hold values from -6 to 6
- image_counts: int32 [32, 32], P(('grp', 'dp')), may hold values from 0 to 98, as said below
- group_of_device: int32 [32], P(('grp', 'dp')), may hold values from 0 to 2, as said below
- group_weight: int32 [3], replicated, may hold values from 1 to 4
- norm1_gain: bfloat16 [768], replicated, may hold values from 0.5 to 1.5
- norm1_bias: bfloat16 [768], replicated, may hold values from -4 to 4
- qkv_weight: bfloat16 [768, 2304], replicated, may hold values from -0.21875 to 0.21875
- qkv_bias: bfloat16 [2304], replicated, may hold values from -4 to 4
- proj_weight: bfloat16 [768, 768], replicated, may hold values from -0.875 to 0.875
- proj_bias: bfloat16 [768], replicated, may hold values from -4 to 4
- norm2_gain: bfloat16 [768], replicated, may hold values from 0.5 to 1.5
- norm2_bias: bfloat16 [768], replicated, may hold values from -4 to 4
- fc1_weight: bfloat16 [768, 3072], replicated, may hold values from -0.21875 to 0.21875
- fc1_bias: bfloat16 [3072], replicated, may hold values from -4 to 4
- fc2_weight: bfloat16 [3072, 768], replicated, may hold values from -0.109375 to 0.109375
- fc2_bias: bfloat16 [768], replicated, may hold values from -4 to 4
- first_moment: float32 [16, 442992], P('dp'), may hold values from -2.5 to 2.5
- second_moment: float32 [16, 442992], P('dp'), may hold values from 1e-05 to 0.001
Outputs:
- block_out: bfloat16 [32768, 768], P(('grp', 'dp'))
- input_grad: bfloat16 [32768, 768], P(('grp', 'dp'))
- weight_grads: float32 [16, 442992], P('dp')
- new_weights: bfloat16 [16, 442992], replicated
- new_first: float32 [16, 442992], P('dp')
- new_second: float32 [16, 442992], P('dp')
- fc2_bias_grad: float32 [768], P('dp')
Inputs may be any that keep to these rules, and one draw needn't show every extreme that they name: `group_of_device`: each of the 3 groups holds some devices: about a half, a third and a sixth of them. `image_counts`: in each device's row the live images come first, at least one, each with 30 to 98 visible patches, summing to at most 1024; the remaining slots are 0.
All inputs are finite; a program needn't handle non-finite values.
Results may differ from a plain program's by a relative error of at most 0.012.
Values may be sent and summed in bfloat16 or wider, within the bound.
No kernel may reach another device: no remote copies, remote signals or barrier semaphores. Data moves between devices by JAX's collectives and lax.ppermute only.
A program may use at most 320 MiB of HBM per device.

v0:
```python
import jax
import jax.numpy as jnp
from jax import lax
from jax.sharding import PartitionSpec as P

D = 768
HEADS = 12
HEAD_DIM = 64
NGROUPS = 3
beta_one = 0.9
beta_two = 0.999
adam_eps = 1e-08
decay_rate = 0.05
step_count = 10.0
learn_rate = 0.004 * 0.75**1
norm_eps = 1e-06
neg_fill = -1e30
decay_flags = (0.0, 0.0, 1.0, 0.0, 1.0, 0.0, 0.0, 0.0, 1.0, 0.0, 1.0, 0.0)


def layer_norm(values, gain, shift):
    center = values - jnp.mean(values, axis=-1, keepdims=True)
    spread = jnp.mean(center * center, axis=-1, keepdims=True)
    return center * lax.rsqrt(spread + norm_eps) * gain + shift


def gelu_tanh(values):
    return jax.nn.gelu(values, approximate=True)


def contract_rows(first_op, second_op):
    return lax.dot_general(
        first_op, second_op, (((0,), (0,)), ((), ())), preferred_element_type=jnp.float32
    )


def contract_cols(first_op, second_op):
    return lax.dot_general(
        first_op, second_op, (((1,), (1,)), ((), ())), preferred_element_type=jnp.float32
    )


def segment_info(counts_row, length):
    segment_ends = jnp.cumsum(counts_row)
    position = lax.iota(jnp.int32, length)
    segment = jnp.sum((position[:, None] >= segment_ends[None, :]).astype(jnp.int32), axis=1)
    return (segment, position < segment_ends[-1])


def score_block(query_part, key_rows, same_segment):
    raw = (
        jnp.einsum("qhd,khd->hqk", query_part, key_rows, preferred_element_type=jnp.float32) * 0.125
    )
    return jnp.where(same_segment[None], raw, neg_fill)


def on_device(
    tokens,
    out_grad,
    image_counts,
    group_of_device,
    group_weight,
    norm1_gain,
    norm1_bias,
    qkv_weight,
    qkv_bias,
    proj_weight,
    proj_bias,
    norm2_gain,
    norm2_bias,
    fc1_weight,
    fc1_bias,
    fc2_weight,
    fc2_bias,
    first_moment,
    second_moment,
):
    length = tokens.shape[0]
    segment, valid_rows = segment_info(image_counts[0], length)
    images = jnp.sum((image_counts[0] > 0).astype(jnp.int32))
    member = (group_of_device[0] == lax.iota(jnp.int32, NGROUPS)).astype(jnp.int32)
    totals = lax.psum(member * images, ("grp", "dp"))
    factor = jnp.sum(member * group_weight).astype(jnp.float32) / jnp.sum(member * totals).astype(
        jnp.float32
    )
    inputs = tokens.astype(jnp.float32)
    normed_one, norm_one_back = jax.vjp(
        layer_norm, inputs, norm1_gain.astype(jnp.float32), norm1_bias.astype(jnp.float32)
    )
    normed_one_low = normed_one.astype(jnp.bfloat16)
    projected = (
        jnp.dot(normed_one_low, qkv_weight, preferred_element_type=jnp.float32)
        + qkv_bias.astype(jnp.float32)
    ).astype(jnp.bfloat16)
    query_rows = projected[:, :D].reshape(length, HEADS, HEAD_DIM)
    key_rows = projected[:, D : 2 * D].reshape(length, HEADS, HEAD_DIM)
    value_rows = projected[:, 2 * D :].reshape(length, HEADS, HEAD_DIM)
    block_rows = min(512, length)
    offsets = list(range(0, length, block_rows))
    context_parts = []
    log_sums = []
    for offset in offsets:
        same_segment = segment[offset : offset + block_rows, None] == segment[None, :]
        scores = score_block(query_rows[offset : offset + block_rows], key_rows, same_segment)
        row_max = jnp.max(scores, axis=-1, keepdims=True)
        exponent = jnp.exp(scores - row_max)
        row_sum = jnp.sum(exponent, axis=-1, keepdims=True)
        attn_probs = exponent / row_sum
        log_sums.append(row_max + jnp.log(row_sum))
        context_parts.append(
            jnp.einsum(
                "hqk,khd->qhd",
                attn_probs.astype(jnp.bfloat16),
                value_rows,
                preferred_element_type=jnp.float32,
            )
        )
    context = jnp.concatenate(context_parts, axis=0).reshape(length, D).astype(jnp.bfloat16)
    middle = inputs + (
        jnp.dot(context, proj_weight, preferred_element_type=jnp.float32)
        + proj_bias.astype(jnp.float32)
    )
    normed_two, norm_two_back = jax.vjp(
        layer_norm, middle, norm2_gain.astype(jnp.float32), norm2_bias.astype(jnp.float32)
    )
    normed_two_low = normed_two.astype(jnp.bfloat16)
    hidden = jnp.dot(
        normed_two_low, fc1_weight, preferred_element_type=jnp.float32
    ) + fc1_bias.astype(jnp.float32)
    activated, gelu_back = jax.vjp(gelu_tanh, hidden)
    activated_low = activated.astype(jnp.bfloat16)
    block_out = (
        middle
        + (
            jnp.dot(activated_low, fc2_weight, preferred_element_type=jnp.float32)
            + fc2_bias.astype(jnp.float32)
        )
    ).astype(jnp.bfloat16)
    grad_out = out_grad.astype(jnp.float32) * valid_rows[:, None].astype(jnp.float32)
    grad_out_low = grad_out.astype(jnp.bfloat16)
    fc2_grad = contract_rows(activated_low, grad_out_low)
    fc2_bias_grad = jnp.sum(grad_out, axis=0)
    grad_hidden = gelu_back(contract_cols(grad_out_low, fc2_weight))[0].astype(jnp.bfloat16)
    fc1_grad = contract_rows(normed_two_low, grad_hidden)
    fc1_bias_grad = jnp.sum(grad_hidden.astype(jnp.float32), axis=0)
    grad_middle_norm, gain_two_grad, shift_two_grad = norm_two_back(
        contract_cols(grad_hidden, fc1_weight)
    )
    grad_middle = grad_out + grad_middle_norm
    grad_branch = grad_middle.astype(jnp.bfloat16)
    proj_grad = contract_rows(context, grad_branch)
    proj_bias_grad = jnp.sum(grad_branch.astype(jnp.float32), axis=0)
    grad_context = (
        contract_cols(grad_branch, proj_weight)
        .astype(jnp.bfloat16)
        .reshape(length, HEADS, HEAD_DIM)
    )
    grad_keys = jnp.zeros((length, HEADS, HEAD_DIM), jnp.float32)
    grad_values = jnp.zeros((length, HEADS, HEAD_DIM), jnp.float32)
    query_grads = []
    for piece_index, offset in enumerate(offsets):
        query_part = query_rows[offset : offset + block_rows]
        context_grad_part = grad_context[offset : offset + block_rows]
        same_segment = segment[offset : offset + block_rows, None] == segment[None, :]
        attn_probs = jnp.exp(
            score_block(query_part, key_rows, same_segment) - log_sums[piece_index]
        )
        grad_probs = jnp.einsum(
            "qhd,khd->hqk", context_grad_part, value_rows, preferred_element_type=jnp.float32
        )
        grad_scores = (
            attn_probs * (grad_probs - jnp.sum(attn_probs * grad_probs, axis=-1, keepdims=True))
        ).astype(jnp.bfloat16)
        query_grads.append(
            jnp.einsum("hqk,khd->qhd", grad_scores, key_rows, preferred_element_type=jnp.float32)
            * 0.125
        )
        grad_keys = (
            grad_keys
            + jnp.einsum(
                "hqk,qhd->khd", grad_scores, query_part, preferred_element_type=jnp.float32
            )
            * 0.125
        )
        grad_values = grad_values + jnp.einsum(
            "hqk,qhd->khd",
            attn_probs.astype(jnp.bfloat16),
            context_grad_part,
            preferred_element_type=jnp.float32,
        )
    grad_projected = jnp.concatenate(
        [
            jnp.concatenate(query_grads, axis=0).reshape(length, D),
            grad_keys.reshape(length, D),
            grad_values.reshape(length, D),
        ],
        axis=1,
    ).astype(jnp.bfloat16)
    qkv_grad = contract_rows(normed_one_low, grad_projected)
    qkv_bias_grad = jnp.sum(grad_projected.astype(jnp.float32), axis=0)
    grad_input_norm, gain_one_grad, shift_one_grad = norm_one_back(
        contract_cols(grad_projected, qkv_weight)
    )
    input_grad = (grad_middle + grad_input_norm).astype(jnp.bfloat16)
    row_count = lax.axis_size("dp")
    grad_list = (
        gain_one_grad,
        shift_one_grad,
        qkv_grad,
        qkv_bias_grad,
        proj_grad,
        proj_bias_grad,
        gain_two_grad,
        shift_two_grad,
        fc1_grad,
        fc1_bias_grad,
        fc2_grad,
        fc2_bias_grad,
    )
    packed = jnp.concatenate(
        [(grad_item * factor).reshape(row_count, -1) for grad_item in grad_list], axis=1
    )
    grad_part = lax.psum_scatter(packed, "dp", scatter_dimension=0, tiled=True)
    summed = lax.psum(grad_part, "grp")
    bias_width = fc2_bias.shape[0] // row_count
    summed_bias = summed[0, summed.shape[1] - bias_width :]
    own_index = lax.axis_index("dp")
    weight_list = (
        norm1_gain,
        norm1_bias,
        qkv_weight,
        qkv_bias,
        proj_weight,
        proj_bias,
        norm2_gain,
        norm2_bias,
        fc1_weight,
        fc1_bias,
        fc2_weight,
        fc2_bias,
    )
    current = jnp.concatenate(
        [
            lax.dynamic_slice_in_dim(weight_item.reshape(row_count, -1), own_index, 1, 0).astype(
                jnp.float32
            )
            for weight_item in weight_list
        ],
        axis=1,
    )
    decay = jnp.concatenate(
        [
            jnp.full((1, weight_item.size // row_count), decay_flag, jnp.float32)
            for weight_item, decay_flag in zip(weight_list, decay_flags)
        ],
        axis=1,
    )
    new_first = beta_one * first_moment + (1.0 - beta_one) * summed
    new_second = beta_two * second_moment + (1.0 - beta_two) * summed * summed
    ratio = (
        new_first
        / (1.0 - beta_one**step_count)
        / (jnp.sqrt(new_second / (1.0 - beta_two**step_count)) + adam_eps)
    )
    fresh_low = (current - learn_rate * (ratio + decay_rate * decay * current)).astype(jnp.bfloat16)
    new_weights = lax.all_gather(fresh_low, "dp", axis=0, tiled=True)
    return (block_out, input_grad, summed, new_weights, new_first, new_second, summed_bias)


def solution(mesh):
    in_specs = (
        P(("grp", "dp"), None),
        P(("grp", "dp"), None),
        P(("grp", "dp"), None),
        P(("grp", "dp")),
        P(),
        P(),
        P(),
        P(),
        P(),
        P(),
        P(),
        P(),
        P(),
        P(),
        P(),
        P(),
        P(),
        P("dp", None),
        P("dp", None),
    )
    out_specs = (
        P(("grp", "dp"), None),
        P(("grp", "dp"), None),
        P("dp", None),
        P(),
        P("dp", None),
        P("dp", None),
        P("dp"),
    )
    return jax.shard_map(
        on_device, mesh=mesh, in_specs=in_specs, out_specs=out_specs, check_vma=False
    )
```

profile of v0, /device:TPU:0, one launch (start us, length us, event | category | flops | bytes accessed | tf_op | source)
XLA Modules:
  0.0 1624.3 jit_solution(11156478044281256966)
XLA Ops:
  10.4 6.4 add_convert_fusion
  22.5 2.9 copy.93
  26.9 12.2 fusion.19
  39.1 11.8 fusion
  51.5 2.6 copy.91
  54.0 12.7 fusion.44
  66.7 2.3 copy.95
  69.0 12.4 fusion.20
  81.4 13.4 fusion.1
  94.9 2.4 copy-done
  97.3 8.5 fusion.45
  111.9 2.7 copy.97
  114.6 10.8 fusion.63
  125.5 16.4 %convert_reduce_fusion = (f32[3072]{0:T(1024)}, bf16[1024,3072]{1,0:T(8,128)(2,1)S(1)}) fusion(f32[1024,3072]{1,0:T(8,128)} %fusion.63, f32[3072]{0:T(1024)S(1)} %convert_element_type.143, bf16[3072,768]{1,0:T(8,128)(2,1)} %param.34, bf16[1024,768]{0,1:T(8,128)(2,1)S(1)} %copy-done.14, f32[1024]{0:T(1024)S(1)} %fusion.47), kind=kOutput, calls=%fused_computation.28 | convolution fusion | flops 4906546176 | bytes 25194496 | tf_op jit(solution)/shard_map/dot_general | solution.py:38
  141.9 7.3 fusion.73
  149.2 3.5 copy.98
  152.8 3.5 multiply_reduce_fusion.2
  162.8 21.6 %multiply_reduce_fusion.1 = (f32[12,512]{1,0:T(8,128)S(1)}, f32[12,512,1024]{2,1,0:T(8,128)}) fusion(f32[12,512]{1,0:T(8,128)S(1)} %copy-done.43, f32[12,512,1024]{2,1,0:T(8,128)} %get-tuple-element.68, pred[512,1024]{1,0:T(8,128)(4,1)S(1)} %copy-done.18, bf16[512,12,64]{0,2,1:T(8,128)(2,1)S(1)} %bitcast.95, bf16[1024,12,64]{0,2,1:T(8,128)(2,1)S(1)} %bitcast.81), kind=kOutput, calls=%fused_computation.4 | convolution fusion | flops 836757504 | bytes 53264384 | tf_op jit(solution)/shard_map/qhd,khd->hqk/dot_general | solution.py:168
  184.4 17.7 %multiply_reduce_fusion = (f32[12,512]{1,0:T(8,128)S(1)}, f32[12,512,1024]{2,1,0:T(8,128)}) fusion(f32[12,512]{1,0:T(8,128)S(1)} %log_add_fusion, f32[12,512,1024]{2,1,0:T(8,128)} %get-tuple-element.66, pred[512,1024]{1,0:T(8,128)(4,1)S(1)} %copy-done.20, bf16[512,12,64]{0,2,1:T(8,128)(2,1)} %bitcast.97, bf16[1024,12,64]{0,2,1:T(8,128)(2,1)S(1)} %bitcast.82), kind=kOutput, calls=%fused_computation.1 | convolution fusion | flops 836757504 | bytes 53264384 | tf_op jit(solution)/shard_map/qhd,khd->hqk/dot_general | solution.py:168
  202.1 42.2 %multiply_convert_fusion = (bf16[12,512,1024]{2,1,0:T(8,128)(2,1)}, bf16[12,512,1024]{2,1,0:T(8,128)(2,1)}) fusion(f32[12,512,1024]{2,1,0:T(8,128)} %get-tuple-element.74, f32[12,512]{1,0:T(8,128)S(1)} %get-tuple-element.73, f32[12,512]{1,0:T(8,128)S(1)} %log_add_fusion, f32[12,512,1024]{2,1,0:T(8,128)} %get-tuple-element.66, ...), kind=kLoop, calls=%fused_computation | loop fusion | flops 75497472 | bytes 126976000 | tf_op jit(solution)/shard_map/convert_element_type | solution.py:173
  244.3 9.6 fusion.42
  253.9 8.8 fusion.74
  262.7 13.3 fusion.11
  276.7 6.3 fusion.43
  283.0 5.6 multiply_convert_fusion.3
  288.6 13.0 add_convert_fusion.2
  301.9 2.3 copy-done.22
  305.3 5.6 fusion.72
  312.1 42.2 %psum.14 = s32[3]{0:T(128)S(1)} all-reduce(s32[3]{0:T(128)S(1)} %fusion.51), channel_id=1, replica_groups=mesh['grp'=2,'dp'=16] {'grp','dp'}, use_global_device_ids=true, to_apply=%region_19.20 | all-reduce | flops 3 | bytes 24 | tf_op jit(solution)/shard_map/psum | solution.py:82
  357.0 9.0 convolution_multiply_fusion
  366.0 2.9 convolution_multiply_fusion.3
  368.9 10.7 convolution_multiply_fusion.2
  379.7 10.9 convolution_multiply_fusion.1
  390.7 5.6 reshape.518
  396.3 4.0 copy.99
  400.3 2.6 fusion.31
  404.6 2.9 reshape.519
  407.8 10.7 reshape.520
  418.6 10.6 reshape.521
  429.2 5.6 fusion.32
  437.7 20.7 %dynamic-update-slice.24 = f32[16,442992]{1,0:T(8,128)} dynamic-update-slice(f32[16,442992]{1,0:T(8,128)} %dynamic-update-slice.23, f32[16,110592]{1,0:T(8,128)} %reshape.518, s32[]{} %constant.87, s32[]{} %constant.88) | dynamic-update-slice | bytes 14155780
  459.9 7.6 dynamic-update-slice.26
  471.9 6.5 constant_dynamic-update-slice_fusion
  479.8 27.0 %dynamic-update-slice.32 = f32[16,442992]{1,0:T(8,128)} dynamic-update-slice(f32[16,442992]{1,0:T(8,128)} %dynamic-update-slice.31, f32[16,147456]{1,0:T(8,128)} %reshape.521, s32[]{} %constant.87, s32[]{} %constant.95) | dynamic-update-slice | bytes 18874372
  510.8 3.3 reshape.524
  514.2 2.5 reshape.526
  518.2 5.2 reshape.530
  523.4 5.2 reshape.532
  533.8 8.7 dynamic-update-slice.1
  544.0 3.8 dynamic-update-slice.3
  555.0 8.8 dynamic-update-slice.12
  565.3 3.7 dynamic-update-slice.14
  573.1 2.0 constant_dynamic-slice_fusion.1
  576.1 667.0 %all-reduce.6.cloned.1.call-done = f32[16,442992]{1,0:T(8,128)} async-done(((f32[16,442992]{1,0:T(8,128)}), f32[16,442992]{1,0:T(8,128)}) %all-reduce.6.cloned.1.call-update) | async-done | bytes 28351504
  1243.1 7.5 constant_dynamic-slice_fusion.11
  1250.8 3.0 dynamic-slice_dynamic-update-slice_fusion
  1255.6 11.4 dynamic-update-slice.8
  1269.6 11.3 dynamic-update-slice.20
  1282.1 14.6 convert_bitcast_fusion
  1296.8 2.7 copy.103
  1299.5 11.8 add_convert_fusion.3
  1311.4 2.6 copy.102
  1315.2 282.6 %all-gather.3.cloned.1.call-done = bf16[16,1,442992]{2,1,0:T(2,128)(2,1)} async-done(((bf16[1,1,442992]{2,1,0:T(2,128)(2,1)}), bf16[16,1,442992]{2,1,0:T(2,128)(2,1)}) %all-gather.3.cloned.1.call-update) | async-done | bytes 14175760 | tf_op jit(solution)/shard_map/all_gather | solution.py:266
  1597.8 18.5 %copy.107 = bf16[16,1,442992]{2,0,1:T(8,128)(2,1)} copy(bf16[16,1,442992]{2,1,0:T(2,128)(2,1)} %all-gather.3.cloned.1.call-done) | data formatting | bytes 28351488
  (297 shorter events, 73.6 us)
Async XLA Ops:
  7.2 3.2 copy-start.68
  7.2 3.2 copy-start.64
  7.2 3.2 copy-start.54
  7.2 1235.9 %all-reduce.6.cloned.1.call-start = ((), (), s32[]{:S(2)}) async-start(), calls=%async_computation.2 | async-start | bytes 56705024
  9.0 98.3 %copy-start.1 = (bf16[1024,768]{0,1:T(8,128)(2,1)}, bf16[1024,768]{0,1:T(8,128)(2,1)S(1)}, u32[]{:S(2)}) copy-start(bf16[1024,768]{0,1:T(8,128)(2,1)S(1)} %copy.90) | copy-start | bytes 4718596
  9.3 7.6 copy-start.44
  10.3 6.5 copy-start.48
  10.3 6.5 copy-start.46
  10.4 6.5 copy-start.73
  22.5 46.6 %copy-start.8 = (bf16[1024,768]{0,1:T(8,128)(2,1)}, bf16[1024,768]{0,1:T(8,128)(2,1)S(1)}, u32[]{:S(2)}) copy-start(bf16[1024,768]{0,1:T(8,128)(2,1)S(1)} %copy.94) | copy-start | bytes 4718596
  26.9 12.2 copy-start.17
  69.0 25.9 %copy-start.12 = (bf16[1024,768]{0,1:T(8,128)(2,1)S(1)}, bf16[1024,768]{0,1:T(8,128)(2,1)}, u32[]{:S(2)}) copy-start(bf16[1024,768]{0,1:T(8,128)(2,1)} %copy.91) | copy-start | bytes 4718596
  81.4 15.8 copy-start
  81.4 15.9 copy-start.19
  97.3 8.5 copy-start.66
  97.3 8.5 copy-start.40
  110.7 3.9 copy-start.56
  111.0 3.5 copy-start.4
  111.1 14.4 copy-start.41
  114.6 10.9 copy-start.60
  114.6 10.9 copy-start.14
  114.6 27.3 %slice-start.3 = ((s8[4718592]{0:T(1024)(128)(4,1)}), s8[4194304]{0:T(1024)(128)(4,1)S(1)}, s32[]{:S(2)}) async-start(s8[4718592]{0:T(1024)(128)(4,1)} %bitcast.76), calls=%async_computation.6 | async-start | bytes 8388608
  125.5 16.4 %slice-start.4 = ((s8[4718592]{0:T(1024)(128)(4,1)}), s8[524288]{0:T(1024)(128)(4,1)S(1)}, s32[]{:S(2)}) async-start(s8[4718592]{0:T(1024)(128)(4,1)} %bitcast.76), calls=%async_computation.7 | async-start | bytes 1048576
  141.9 7.3 copy-start.79
  152.8 3.5 copy-start.11
  162.0 22.4 %copy-start.30 = (bf16[512,768]{0,1:T(8,128)(2,1)}, bf16[512,768]{0,1:T(8,128)(2,1)S(1)}, u32[]{:S(2)}) copy-start(bf16[512,768]{0,1:T(8,128)(2,1)S(1)} %get-tuple-element.59) | copy-start | bytes 2359300
  162.8 21.7 %copy-start.20 = (pred[512,1024]{1,0:T(8,128)(4,1)S(1)}, pred[512,1024]{1,0:T(8,128)(4,1)}, u32[]{:S(2)}) copy-start(pred[512,1024]{1,0:T(8,128)(4,1)} %get-tuple-element.62) | copy-start | bytes 1572868
  202.1 42.2 %copy-start.9 = (bf16[1024,768]{0,1:T(8,128)(2,1)S(1)}, bf16[1024,768]{0,1:T(8,128)(2,1)}, u32[]{:S(2)}) copy-start(bf16[1024,768]{0,1:T(8,128)(2,1)} %copy-done.8) | copy-start | bytes 4718596
  244.3 9.6 copy-start.24
  253.9 8.8 copy-start.21
  253.9 8.8 copy-start.31
  253.9 22.7 %slice-start = ((s8[12582912]{0:T(1024)(128)(4,1)}), s8[4194304]{0:T(1024)(128)(4,1)S(1)}, s32[]{:S(2)}) async-start(s8[12582912]{0:T(1024)(128)(4,1)} %bitcast.70), calls=%async_computation.3 | async-start | bytes 8388608
  253.9 22.7 %slice-start.1 = ((s8[12582912]{0:T(1024)(128)(4,1)}), s8[4194304]{0:T(1024)(128)(4,1)S(1)}, s32[]{:S(2)}) async-start(s8[12582912]{0:T(1024)(128)(4,1)} %bitcast.70), calls=%async_computation.4 | async-start | bytes 8388608
  262.7 13.3 copy-start.77
  262.7 13.9 slice-start.2
  288.6 13.1 copy-start.28
  288.6 13.1 copy-start.29
  301.6 3.3 copy-start.37
  301.8 9.0 copy-start.26
  301.9 3.4 copy-start.27
  305.3 50.3 %copy-start.78 = (s32[3]{0:T(128)S(1)}, s32[3]{0:T(128)}, u32[]{:S(2)}) copy-start(s32[3]{0:T(128)} %param.23) | copy-start | bytes 40
  305.3 51.7 %copy-start.2 = (bf16[1024,768]{0,1:T(8,128)(2,1)S(1)}, bf16[1024,768]{0,1:T(8,128)(2,1)}, u32[]{:S(2)}) copy-start(bf16[1024,768]{0,1:T(8,128)(2,1)} %copy-done.1) | copy-start | bytes 4718596
  305.3 51.7 %copy-start.45 = (f32[1024]{0:T(1024)S(1)}, f32[1024]{0:T(1024)}, u32[]{:S(2)}) copy-start(f32[1024]{0:T(1024)} %copy-done.44) | copy-start | bytes 12292
  305.3 51.7 %copy-start.47 = (f32[768]{0:T(1024)S(1)}, f32[768]{0:T(1024)}, u32[]{:S(2)}) copy-start(f32[768]{0:T(1024)} %copy-done.46) | copy-start | bytes 9220
  305.3 51.7 %copy-start.49 = (f32[1024]{0:T(1024)S(1)}, f32[1024]{0:T(1024)}, u32[]{:S(2)}) copy-start(f32[1024]{0:T(1024)} %copy-done.48) | copy-start | bytes 12292
  305.3 51.7 %copy-start.74 = (f32[768]{0:T(1024)S(1)}, f32[768]{0:T(1024)}, u32[]{:S(2)}) copy-start(f32[768]{0:T(1024)} %copy-done.73) | copy-start | bytes 9220
  357.0 9.0 copy-start.34
  357.0 9.0 copy-start.36
  366.0 13.7 slice-start.5
  368.9 10.8 copy-start.16
  368.9 10.8 slice-start.6
  368.9 10.8 slice-start.7
  368.9 10.8 copy-start.61
  404.4 3.2 copy-start.59
  407.8 10.7 copy-start.63
  418.6 10.7 copy-start.53
  437.7 22.2 %copy-start.23 = (f32[16,36864]{1,0:T(8,128)S(1)}, f32[16,36864]{1,0:T(8,128)}, u32[]{:S(2)}) copy-start(f32[16,36864]{1,0:T(8,128)} %reshape.519) | copy-start | bytes 7077892
  508.1 774.0 %all-reduce.4.cloned.1.call-start = ((), (), s32[]{:S(2)}) async-start(), calls=%async_computation | async-start | bytes 3544064 | tf_op jit(solution)/shard_map/psum | solution.py:224
  510.8 3.3 copy-start.55
  1243.1 10.7 copy-start.57
  1243.1 10.7 copy-start.72
  1250.7 31.4 %copy-start.32 = (f32[1,442992]{1,0:T(1,128)S(1)}, f32[1,442992]{1,0:T(1,128)}, u32[]{:S(2)}) copy-start(f32[1,442992]{1,0:T(1,128)} %param.36) | copy-start | bytes 5315908
  1250.7 347.1 %all-gather.3.cloned.1.call-start = ((), (), s32[]{:S(2)}) async-start(), calls=%async_computation.1 | async-start | bytes 30124544 | tf_op jit(solution)/shard_map/all_gather | solution.py:266
  1315.2 301.2 %copy-start.25 = (f32[1,442992]{1,0:T(1,128)S(1)}, f32[1,442992]{1,0:T(1,128)}, u32[]{:S(2)}) copy-start(f32[1,442992]{1,0:T(1,128)} %all-reduce.4.cloned.1.call-done) | copy-start | bytes 5315908
  (27 other events, 54.6 us)
Sparse Core Ops, SparseCore 0:
  508.2 734.8 all-reduce.5
  1250.8 19.8 all-reduce.3
  1296.9 300.8 all-gather.2
where the time goes:
time: 1640 us; the launch traced here: 1620 us
  waiting for transfers between devices  950 us (58%)
  local copies, waits for them, and re-layouts  272 us (17%)
  matrix products  237 us (14%)
  other arithmetic  106 us (6%)
  blocking collectives  42.2 us (3%)
  between operations  17 us (1%)
    unnamed x4, waiting for transfers between devices  667 us
    all_gather x1, waiting for transfers between devices, on_device(): new_weights = lax.all_gather(fresh_low, 'dp', axis=0, tiled=True)  283 us
    unnamed x215, local copies, waits for them, and re-layouts  188 us
    psum x1, blocking collectives, on_device(): totals = lax.psum(member * images, ('grp', 'dp'))  42.2 us
    convert_element_type x1, other arithmetic, on_device(): grad_scores = (attn_probs * (grad_probs - jnp.sum(attn_probs * grad_probs...  42.2 us
    dot_general x2, matrix products, on_device(): jnp.einsum('qhd,khd->hqk', context_grad_part, value_rows, preferred_eleme...  39.4 us
    dot_general x4, matrix products, contract_rows(): lax.dot_general(first_op, second_op, (((0,), (0,)), ((), ())), preferred_...  33.5 us
  transfers between devices with their start and end apart: 3, of which 2 were waited for; matrix products, arithmetic and copies ran while one was open for 7% of the time, Pallas kernels for 0%

commit v1 on v0

--- a/solution.py
+++ b/solution.py
@@ -263,7 +263,12 @@
         / (jnp.sqrt(new_second / (1.0 - beta_two**step_count)) + adam_eps)
     )
     fresh_low = (current - learn_rate * (ratio + decay_rate * decay * current)).astype(jnp.bfloat16)
-    new_weights = lax.all_gather(fresh_low, "dp", axis=0, tiled=True)
+    ring = [fresh_low]
+    for hop in range(15):
+        ring.append(lax.ppermute(ring[-1], "dp", [(dev, (dev + 1) % 16) for dev in range(16)]))
+    new_weights = jnp.roll(
+        jnp.concatenate(ring[::-1], axis=0), (lax.axis_index("dp") + 1) * ring[0].shape[0], axis=0
+    )
     return (block_out, input_grad, summed, new_weights, new_first, new_second, summed_bias)
 
 

time: 1640 us -> 2100 us (1.28)
  waiting for transfers between devices: 950 us -> 1230 us
  local copies, waits for them, and re-layouts: 272 us -> 434 us
    ppermute x0 -> x15, waiting for transfers between devices: none -> 565 us  [on_device(): lax.ppermute(ring[-1], 'dp', [(dev, (dev + 1) % 16) for dev in range(16)])]
    all_gather x1 -> x0, waiting for transfers between devices: 283 us -> none  [on_device(): new_weights = lax.all_gather(fresh_low, 'dp', axis=0, tiled=True)]
    concatenate x0 -> x1, local copies, waits for them, and re-layouts: none -> 148 us  [on_device(): jnp.roll(jnp.concatenate(ring[::-1], axis=0), (lax.axis_index('dp') + 1)...]
    unnamed x215 -> x244, local copies, waits for them, and re-layouts: 188 us -> 186 us
    unnamed x4 -> x3, waiting for transfers between devices: 667 us -> 667 us
  transfers between devices with their start and end apart: 3 -> 17, of which waited for: 2 -> 16; matrix products, arithmetic and copies ran while one was open for 7% -> 6% of each run, Pallas kernels for 0% -> 0%
where the time goes in v1:
time: 2100 us; the launch traced here: 2070 us
  waiting for transfers between devices  1230 us (59%)
  local copies, waits for them, and re-layouts  434 us (21%)
  matrix products  237 us (11%)
  other arithmetic  107 us (5%)
  blocking collectives  42.3 us (2%)
    unnamed x3, waiting for transfers between devices  667 us
    ppermute x15, waiting for transfers between devices, on_device(): lax.ppermute(ring[-1], 'dp', [(dev, (dev + 1) % 16) for dev in range(16)])  565 us
    unnamed x244, local copies, waits for them, and re-layouts  186 us
    concatenate x1, local copies, waits for them, and re-layouts, on_device(): jnp.roll(jnp.concatenate(ring[::-1], axis=0), (lax.axis_index('dp') + 1)...  148 us
    psum x1, blocking collectives, on_device(): totals = lax.psum(member * images, ('grp', 'dp'))  42.3 us
    convert_element_type x1, other arithmetic, on_device(): grad_scores = (attn_probs * (grad_probs - jnp.sum(attn_probs * grad_probs...  42.2 us
  transfers between devices with their start and end apart: 17, of which 16 were waited for; matrix products, arithmetic and copies ran while one was open for 6% of the time, Pallas kernels for 0%

profile of v1, /device:TPU:0, one launch (start us, length us, event | category | flops | bytes accessed | tf_op | source)
XLA Modules:
  0.0 2070.3 jit_solution(16985247987183845828)
XLA Ops:
  10.4 6.4 add_convert_fusion
  26.9 12.1 fusion.19
  39.0 11.8 fusion
  54.0 12.7 fusion.44
  69.0 12.6 fusion.20
  81.5 13.4 fusion.1
  97.4 8.5 fusion.45
  114.8 10.8 fusion.63
  125.6 16.4 convert_reduce_fusion
  142.0 7.4 fusion.73
  149.4 3.5 copy.84
  152.9 3.5 multiply_reduce_fusion.2
  162.9 21.7 %multiply_reduce_fusion.1 = (f32[12,512]{1,0:T(8,128)S(1)}, f32[12,512,1024]{2,1,0:T(8,128)}) fusion(f32[12,512]{1,0:T(8,128)S(1)} %copy-done.58, f32[12,512,1024]{2,1,0:T(8,128)} %get-tuple-element.61, pred[512,1024]{1,0:T(8,128)(4,1)S(1)} %copy-done.20, bf16[512,12,64]{0,2,1:T(8,128)(2,1)S(1)} %bitcast.89, bf16[1024,12,64]{0,2,1:T(8,128)(2,1)S(1)} %bitcast.75), kind=kOutput, calls=%fused_computation.4 | convolution fusion | flops 836757504 | bytes 53264384 | tf_op jit(solution)/shard_map/qhd,khd->hqk/dot_general | solution.py:168
  184.6 17.8 multiply_reduce_fusion
  202.4 42.2 %multiply_convert_fusion = (bf16[12,512,1024]{2,1,0:T(8,128)(2,1)}, bf16[12,512,1024]{2,1,0:T(8,128)(2,1)}) fusion(f32[12,512,1024]{2,1,0:T(8,128)} %get-tuple-element.67, f32[12,512]{1,0:T(8,128)S(1)} %get-tuple-element.66, f32[12,512]{1,0:T(8,128)S(1)} %log_add_fusion, f32[12,512,1024]{2,1,0:T(8,128)} %get-tuple-element.59, ...), kind=kLoop, calls=%fused_computation | loop fusion | flops 75497472 | bytes 126976000 | tf_op jit(solution)/shard_map/convert_element_type | solution.py:173
  244.6 9.6 fusion.42
  254.2 8.8 fusion.74
  263.1 13.3 fusion.11
  277.1 6.3 fusion.43
  283.4 5.6 multiply_convert_fusion.3
  289.0 13.1 add_convert_fusion.2
  305.7 5.5 fusion.72
  312.6 42.3 %psum.14 = s32[3]{0:T(128)S(1)} all-reduce(s32[3]{0:T(128)S(1)} %fusion.51), channel_id=1, replica_groups=mesh['grp'=2,'dp'=16] {'grp','dp'}, use_global_device_ids=true, to_apply=%region_19.20 | all-reduce | flops 3 | bytes 24 | tf_op jit(solution)/shard_map/psum | solution.py:82
  357.5 9.0 convolution_multiply_fusion
  369.4 10.8 convolution_multiply_fusion.2
  380.2 10.9 convolution_multiply_fusion.1
  391.2 5.6 reshape.518
  396.8 3.9 copy.85
  408.2 10.7 reshape.520
  419.0 10.7 reshape.521
  429.8 5.6 fusion.32
  438.3 20.7 dynamic-update-slice.24
  460.5 7.6 dynamic-update-slice.26
  472.4 6.5 constant_dynamic-update-slice_fusion
  480.3 26.9 %dynamic-update-slice.32 = f32[16,442992]{1,0:T(8,128)} dynamic-update-slice(f32[16,442992]{1,0:T(8,128)} %dynamic-update-slice.31, f32[16,147456]{1,0:T(8,128)} %reshape.521, s32[]{} %constant.109, s32[]{} %constant.117) | dynamic-update-slice | bytes 18874372
  518.7 5.2 reshape.530
  523.9 5.2 reshape.532
  534.3 8.7 dynamic-update-slice.1
  544.5 3.8 dynamic-update-slice.3
  555.6 8.8 dynamic-update-slice.12
  565.8 3.7 dynamic-update-slice.14
  576.7 667.0 %all-reduce.6.cloned.1.call-done = f32[16,442992]{1,0:T(8,128)} async-done(((f32[16,442992]{1,0:T(8,128)}), f32[16,442992]{1,0:T(8,128)}) %all-reduce.6.cloned.1.call-update) | async-done | bytes 28351504
  1243.7 7.5 constant_dynamic-slice_fusion.12
  1255.7 11.4 dynamic-update-slice.8
  1269.7 11.3 dynamic-update-slice.20
  1282.3 14.9 subtract_convert_fusion
  1299.8 42.5 %collective-permute-done = bf16[1,442992]{1,0:T(2,128)(2,1)S(1)} collective-permute-done((bf16[1,442992]{1,0:T(2,128)(2,1)S(1)}, bf16[1,442992]{1,0:T(2,128)(2,1)S(1)}, u32[]{:S(2)}, u32[]{:S(2)}) %collective-permute-start) | collective-permute-done | bytes 886016 | tf_op jit(solution)/shard_map/ppermute | solution.py:268
  1343.5 43.0 %collective-permute-done.1 = bf16[1,442992]{1,0:T(2,128)(2,1)S(1)} collective-permute-done((bf16[1,442992]{1,0:T(2,128)(2,1)S(1)}, bf16[1,442992]{1,0:T(2,128)(2,1)S(1)}, u32[]{:S(2)}, u32[]{:S(2)}) %collective-permute-start.1) | collective-permute-done | bytes 886016 | tf_op jit(solution)/shard_map/ppermute | solution.py:268
  1387.8 42.1 %collective-permute-done.2 = bf16[1,442992]{1,0:T(2,128)(2,1)S(1)} collective-permute-done((bf16[1,442992]{1,0:T(2,128)(2,1)S(1)}, bf16[1,442992]{1,0:T(2,128)(2,1)S(1)}, u32[]{:S(2)}, u32[]{:S(2)}) %collective-permute-start.2) | collective-permute-done | bytes 886016 | tf_op jit(solution)/shard_map/ppermute | solution.py:268
  1431.2 41.2 %collective-permute-done.3 = bf16[1,442992]{1,0:T(2,128)(2,1)S(1)} collective-permute-done((bf16[1,442992]{1,0:T(2,128)(2,1)S(1)}, bf16[1,442992]{1,0:T(2,128)(2,1)S(1)}, u32[]{:S(2)}, u32[]{:S(2)}) %collective-permute-start.3) | collective-permute-done | bytes 886016 | tf_op jit(solution)/shard_map/ppermute | solution.py:268
  1473.6 40.3 %collective-permute-done.4 = bf16[1,442992]{1,0:T(2,128)(2,1)S(1)} collective-permute-done((bf16[1,442992]{1,0:T(2,128)(2,1)S(1)}, bf16[1,442992]{1,0:T(2,128)(2,1)S(1)}, u32[]{:S(2)}, u32[]{:S(2)}) %collective-permute-start.4) | collective-permute-done | bytes 886016 | tf_op jit(solution)/shard_map/ppermute | solution.py:268
  1515.1 39.3 %collective-permute-done.5 = bf16[1,442992]{1,0:T(2,128)(2,1)S(1)} collective-permute-done((bf16[1,442992]{1,0:T(2,128)(2,1)S(1)}, bf16[1,442992]{1,0:T(2,128)(2,1)S(1)}, u32[]{:S(2)}, u32[]{:S(2)}) %collective-permute-start.5) | collective-permute-done | bytes 886016 | tf_op jit(solution)/shard_map/ppermute | solution.py:268
  1555.7 38.4 %collective-permute-done.6 = bf16[1,442992]{1,0:T(2,128)(2,1)S(1)} collective-permute-done((bf16[1,442992]{1,0:T(2,128)(2,1)S(1)}, bf16[1,442992]{1,0:T(2,128)(2,1)S(1)}, u32[]{:S(2)}, u32[]{:S(2)}) %collective-permute-start.6) | collective-permute-done | bytes 886016 | tf_op jit(solution)/shard_map/ppermute | solution.py:268
  1595.4 37.6 %collective-permute-done.7 = bf16[1,442992]{1,0:T(2,128)(2,1)S(1)} collective-permute-done((bf16[1,442992]{1,0:T(2,128)(2,1)S(1)}, bf16[1,442992]{1,0:T(2,128)(2,1)S(1)}, u32[]{:S(2)}, u32[]{:S(2)}) %collective-permute-start.7) | collective-permute-done | bytes 886016 | tf_op jit(solution)/shard_map/ppermute | solution.py:268
  1634.2 37.6 %collective-permute-done.8 = bf16[1,442992]{1,0:T(2,128)(2,1)S(1)} collective-permute-done((bf16[1,442992]{1,0:T(2,128)(2,1)S(1)}, bf16[1,442992]{1,0:T(2,128)(2,1)S(1)}, u32[]{:S(2)}, u32[]{:S(2)}) %collective-permute-start.8) | collective-permute-done | bytes 886016 | tf_op jit(solution)/shard_map/ppermute | solution.py:268
  1673.0 37.6 %collective-permute-done.9 = bf16[1,442992]{1,0:T(2,128)(2,1)S(1)} collective-permute-done((bf16[1,442992]{1,0:T(2,128)(2,1)S(1)}, bf16[1,442992]{1,0:T(2,128)(2,1)S(1)}, u32[]{:S(2)}, u32[]{:S(2)}) %collective-permute-start.9) | collective-permute-done | bytes 886016 | tf_op jit(solution)/shard_map/ppermute | solution.py:268
  1711.8 37.6 %collective-permute-done.10 = bf16[1,442992]{1,0:T(2,128)(2,1)S(1)} collective-permute-done((bf16[1,442992]{1,0:T(2,128)(2,1)S(1)}, bf16[1,442992]{1,0:T(2,128)(2,1)S(1)}, u32[]{:S(2)}, u32[]{:S(2)}) %collective-permute-start.10) | collective-permute-done | bytes 886016 | tf_op jit(solution)/shard_map/ppermute | solution.py:268
  1750.7 37.6 %collective-permute-done.11 = bf16[1,442992]{1,0:T(2,128)(2,1)S(1)} collective-permute-done((bf16[1,442992]{1,0:T(2,128)(2,1)S(1)}, bf16[1,442992]{1,0:T(2,128)(2,1)S(1)}, u32[]{:S(2)}, u32[]{:S(2)}) %collective-permute-start.11) | collective-permute-done | bytes 886016 | tf_op jit(solution)/shard_map/ppermute | solution.py:268
  1789.5 37.6 %collective-permute-done.12 = bf16[1,442992]{1,0:T(2,128)(2,1)S(1)} collective-permute-done((bf16[1,442992]{1,0:T(2,128)(2,1)S(1)}, bf16[1,442992]{1,0:T(2,128)(2,1)S(1)}, u32[]{:S(2)}, u32[]{:S(2)}) %collective-permute-start.12) | collective-permute-done | bytes 886016 | tf_op jit(solution)/shard_map/ppermute | solution.py:268
  1828.3 38.6 %collective-permute-done.13 = bf16[1,442992]{1,0:T(2,128)(2,1)} collective-permute-done((bf16[1,442992]{1,0:T(2,128)(2,1)S(1)}, bf16[1,442992]{1,0:T(2,128)(2,1)}, u32[]{:S(2)}, u32[]{:S(2)}) %collective-permute-start.13) | collective-permute-done | bytes 886016 | tf_op jit(solution)/shard_map/ppermute | solution.py:268
  1867.0 11.8 add_convert_fusion.3
  1885.3 13.5 collective-permute-done.14
  1898.8 147.6 %concatenate.62 = bf16[32,442992]{1,0:T(8,128)(2,1)} concatenate(bf16[1,442992]{1,0:T(2,128)(2,1)} %collective-permute-done.14, bf16[1,442992]{1,0:T(2,128)(2,1)} %collective-permute-done.13, bf16[1,442992]{1,0:T(2,128)(2,1)} %copy-done.40, bf16[1,442992]{1,0:T(2,128)(2,1)} %copy-done.39, bf16[1,442992]{1,0:T(2,128)(2,1)} %copy-done.38, bf16[1,442992]{1,0:T(2,128)(2,1)} %copy-done.37, ...), dimensions={0} | concatenate | bytes 56702976 | tf_op jit(solution)/shard_map/jit(_roll_dynamic)/concatenate | solution.py:269
  2046.4 15.6 constant_dynamic-slice_fusion
  (355 shorter events, 131.7 us)
Async XLA Ops:
  7.2 1236.5 %all-reduce.6.cloned.1.call-start = ((), (), s32[]{:S(2)}) async-start(), calls=%async_computation.1 | async-start | bytes 56705024
  9.0 98.4 %copy-start.1 = (bf16[1024,768]{0,1:T(8,128)(2,1)}, bf16[1024,768]{0,1:T(8,128)(2,1)S(1)}, u32[]{:S(2)}) copy-start(bf16[1024,768]{0,1:T(8,128)(2,1)S(1)} %copy.76) | copy-start | bytes 4718596
  22.5 46.5 %copy-start.8 = (bf16[1024,768]{0,1:T(8,128)(2,1)}, bf16[1024,768]{0,1:T(8,128)(2,1)S(1)}, u32[]{:S(2)}) copy-start(bf16[1024,768]{0,1:T(8,128)(2,1)S(1)} %copy.80) | copy-start | bytes 4718596
  26.9 12.1 copy-start.19
  69.0 26.0 %copy-start.14 = (bf16[1024,768]{0,1:T(8,128)(2,1)S(1)}, bf16[1024,768]{0,1:T(8,128)(2,1)}, u32[]{:S(2)}) copy-start(bf16[1024,768]{0,1:T(8,128)(2,1)} %copy.77) | copy-start | bytes 4718596
  81.5 15.8 copy-start
  81.5 15.9 copy-start.21
  111.2 14.4 copy-start.56
  114.7 10.9 copy-start.75
  114.7 10.9 copy-start.16
  114.7 27.3 %slice-start.3 = ((s8[4718592]{0:T(1024)(128)(4,1)}), s8[4194304]{0:T(1024)(128)(4,1)S(1)}, s32[]{:S(2)}) async-start(s8[4718592]{0:T(1024)(128)(4,1)} %bitcast.71), calls=%async_computation.5 | async-start | bytes 8388608
  125.6 16.4 slice-start.4
  162.1 22.5 %copy-start.46 = (bf16[512,768]{0,1:T(8,128)(2,1)}, bf16[512,768]{0,1:T(8,128)(2,1)S(1)}, u32[]{:S(2)}) copy-start(bf16[512,768]{0,1:T(8,128)(2,1)S(1)} %get-tuple-element.52) | copy-start | bytes 2359300
  162.9 21.7 %copy-start.22 = (pred[512,1024]{1,0:T(8,128)(4,1)S(1)}, pred[512,1024]{1,0:T(8,128)(4,1)}, u32[]{:S(2)}) copy-start(pred[512,1024]{1,0:T(8,128)(4,1)} %get-tuple-element.55) | copy-start | bytes 1572868
  202.4 42.2 %copy-start.9 = (bf16[1024,768]{0,1:T(8,128)(2,1)S(1)}, bf16[1024,768]{0,1:T(8,128)(2,1)}, u32[]{:S(2)}) copy-start(bf16[1024,768]{0,1:T(8,128)(2,1)} %copy-done.8) | copy-start | bytes 4718596
  244.6 9.6 copy-start.26
  254.2 8.8 copy-start.23
  254.2 8.8 copy-start.47
  254.2 22.9 %slice-start = ((s8[12582912]{0:T(1024)(128)(4,1)}), s8[4194304]{0:T(1024)(128)(4,1)S(1)}, s32[]{:S(2)}) async-start(s8[12582912]{0:T(1024)(128)(4,1)} %bitcast.65), calls=%async_computation.2 | async-start | bytes 8388608
  254.2 22.9 %slice-start.1 = ((s8[12582912]{0:T(1024)(128)(4,1)}), s8[4194304]{0:T(1024)(128)(4,1)S(1)}, s32[]{:S(2)}) async-start(s8[12582912]{0:T(1024)(128)(4,1)} %bitcast.65), calls=%async_computation.3 | async-start | bytes 8388608
  263.0 13.3 copy-start.92
  263.0 14.0 slice-start.2
  288.9 13.1 copy-start.44
  289.0 13.1 copy-start.45
  302.2 9.0 copy-start.42
  305.7 50.5 %copy-start.93 = (s32[3]{0:T(128)S(1)}, s32[3]{0:T(128)}, u32[]{:S(2)}) copy-start(s32[3]{0:T(128)} %param.23) | copy-start | bytes 40
  305.7 51.8 %copy-start.2 = (bf16[1024,768]{0,1:T(8,128)(2,1)S(1)}, bf16[1024,768]{0,1:T(8,128)(2,1)}, u32[]{:S(2)}) copy-start(bf16[1024,768]{0,1:T(8,128)(2,1)} %copy-done.1) | copy-start | bytes 4718596
  305.7 51.8 %copy-start.60 = (f32[1024]{0:T(1024)S(1)}, f32[1024]{0:T(1024)}, u32[]{:S(2)}) copy-start(f32[1024]{0:T(1024)} %copy-done.59) | copy-start | bytes 12292
  305.7 51.8 %copy-start.62 = (f32[768]{0:T(1024)S(1)}, f32[768]{0:T(1024)}, u32[]{:S(2)}) copy-start(f32[768]{0:T(1024)} %copy-done.61) | copy-start | bytes 9220
  305.7 51.8 %copy-start.64 = (f32[1024]{0:T(1024)S(1)}, f32[1024]{0:T(1024)}, u32[]{:S(2)}) copy-start(f32[1024]{0:T(1024)} %copy-done.63) | copy-start | bytes 12292
  305.7 51.8 %copy-start.89 = (f32[768]{0:T(1024)S(1)}, f32[768]{0:T(1024)}, u32[]{:S(2)}) copy-start(f32[768]{0:T(1024)} %copy-done.88) | copy-start | bytes 9220
  357.5 9.0 copy-start.49
  357.5 9.0 copy-start.51
  366.5 13.7 slice-start.5
  369.4 10.8 copy-start.18
  369.4 10.8 slice-start.6
  369.4 10.8 slice-start.7
  369.4 10.8 copy-start.76
  408.2 10.7 copy-start.78
  419.0 10.7 copy-start.68
  438.3 22.2 %copy-start.25 = (f32[16,36864]{1,0:T(8,128)S(1)}, f32[16,36864]{1,0:T(8,128)}, u32[]{:S(2)}) copy-start(f32[16,36864]{1,0:T(8,128)} %reshape.519) | copy-start | bytes 7077892
  508.7 773.6 %all-reduce.4.cloned.1.call-start = ((), (), s32[]{:S(2)}) async-start(), calls=%async_computation | async-start | bytes 3544064 | tf_op jit(solution)/shard_map/psum | solution.py:224
  1243.7 10.2 copy-start.72
  1243.7 10.3 copy-start.87
  1282.3 584.7 %copy-start.6 = (f32[1024,768]{0,1:T(8,128)S(1)}, f32[1024,768]{0,1:T(8,128)}, u32[]{:S(2)}) copy-start(f32[1024,768]{0,1:T(8,128)} %copy-done.3) | copy-start | bytes 9437188
  1282.3 584.7 %copy-start.77 = (f32[3072]{0:T(1024)S(1)}, f32[3072]{0:T(1024)}, u32[]{:S(2)}) copy-start(f32[3072]{0:T(1024)} %copy-done.75) | copy-start | bytes 36868
  1298.4 43.9 %collective-permute-start = (bf16[1,442992]{1,0:T(2,128)(2,1)S(1)}, bf16[1,442992]{1,0:T(2,128)(2,1)S(1)}, u32[]{:S(2)}, u32[]{:S(2)}) collective-permute-start(bf16[1,442992]{1,0:T(2,128)(2,1)S(1)} %get-tuple-element.39), channel_id=1, source_target_pairs={{0,1},{1,2},{2,3},{3,4},{4,5},{5,6},{6,7},{7,8},{8,9},{9,10},{10,1... | collective-permute-start | bytes 2657960 | tf_op jit(solution)/shard_map/ppermute | solution.py:268
  1343.5 43.0 %collective-permute-start.1 = (bf16[1,442992]{1,0:T(2,128)(2,1)S(1)}, bf16[1,442992]{1,0:T(2,128)(2,1)S(1)}, u32[]{:S(2)}, u32[]{:S(2)}) collective-permute-start(bf16[1,442992]{1,0:T(2,128)(2,1)S(1)} %collective-permute-done), channel_id=1, source_target_pairs={{0,1},{1,2},{2,3},{3,4},{4,5},{5,6},{6,7},{7,8},{8,9},{9,10},{10,1... | collective-permute-start | bytes 2657960 | tf_op jit(solution)/shard_map/ppermute | solution.py:268
  1387.8 42.1 %collective-permute-start.2 = (bf16[1,442992]{1,0:T(2,128)(2,1)S(1)}, bf16[1,442992]{1,0:T(2,128)(2,1)S(1)}, u32[]{:S(2)}, u32[]{:S(2)}) collective-permute-start(bf16[1,442992]{1,0:T(2,128)(2,1)S(1)} %collective-permute-done.1), channel_id=1, source_target_pairs={{0,1},{1,2},{2,3},{3,4},{4,5},{5,6},{6,7},{7,8},{8,9},{9,10},{10,1... | collective-permute-start | bytes 2657960 | tf_op jit(solution)/shard_map/ppermute | solution.py:268
  1431.2 41.2 %collective-permute-start.3 = (bf16[1,442992]{1,0:T(2,128)(2,1)S(1)}, bf16[1,442992]{1,0:T(2,128)(2,1)S(1)}, u32[]{:S(2)}, u32[]{:S(2)}) collective-permute-start(bf16[1,442992]{1,0:T(2,128)(2,1)S(1)} %collective-permute-done.2), channel_id=1, source_target_pairs={{0,1},{1,2},{2,3},{3,4},{4,5},{5,6},{6,7},{7,8},{8,9},{9,10},{10,1... | collective-permute-start | bytes 2657960 | tf_op jit(solution)/shard_map/ppermute | solution.py:268
  1473.6 40.3 %collective-permute-start.4 = (bf16[1,442992]{1,0:T(2,128)(2,1)S(1)}, bf16[1,442992]{1,0:T(2,128)(2,1)S(1)}, u32[]{:S(2)}, u32[]{:S(2)}) collective-permute-start(bf16[1,442992]{1,0:T(2,128)(2,1)S(1)} %collective-permute-done.3), channel_id=1, source_target_pairs={{0,1},{1,2},{2,3},{3,4},{4,5},{5,6},{6,7},{7,8},{8,9},{9,10},{10,1... | collective-permute-start | bytes 2657960 | tf_op jit(solution)/shard_map/ppermute | solution.py:268
  1515.1 39.4 %collective-permute-start.5 = (bf16[1,442992]{1,0:T(2,128)(2,1)S(1)}, bf16[1,442992]{1,0:T(2,128)(2,1)S(1)}, u32[]{:S(2)}, u32[]{:S(2)}) collective-permute-start(bf16[1,442992]{1,0:T(2,128)(2,1)S(1)} %collective-permute-done.4), channel_id=1, source_target_pairs={{0,1},{1,2},{2,3},{3,4},{4,5},{5,6},{6,7},{7,8},{8,9},{9,10},{10,1... | collective-permute-start | bytes 2657960 | tf_op jit(solution)/shard_map/ppermute | solution.py:268
  1555.7 38.4 %collective-permute-start.6 = (bf16[1,442992]{1,0:T(2,128)(2,1)S(1)}, bf16[1,442992]{1,0:T(2,128)(2,1)S(1)}, u32[]{:S(2)}, u32[]{:S(2)}) collective-permute-start(bf16[1,442992]{1,0:T(2,128)(2,1)S(1)} %collective-permute-done.5), channel_id=1, source_target_pairs={{0,1},{1,2},{2,3},{3,4},{4,5},{5,6},{6,7},{7,8},{8,9},{9,10},{10,1... | collective-permute-start | bytes 2657960 | tf_op jit(solution)/shard_map/ppermute | solution.py:268
  1595.4 37.6 %collective-permute-start.7 = (bf16[1,442992]{1,0:T(2,128)(2,1)S(1)}, bf16[1,442992]{1,0:T(2,128)(2,1)S(1)}, u32[]{:S(2)}, u32[]{:S(2)}) collective-permute-start(bf16[1,442992]{1,0:T(2,128)(2,1)S(1)} %collective-permute-done.6), channel_id=1, source_target_pairs={{0,1},{1,2},{2,3},{3,4},{4,5},{5,6},{6,7},{7,8},{8,9},{9,10},{10,1... | collective-permute-start | bytes 2657960 | tf_op jit(solution)/shard_map/ppermute | solution.py:268
  1634.2 37.6 %collective-permute-start.8 = (bf16[1,442992]{1,0:T(2,128)(2,1)S(1)}, bf16[1,442992]{1,0:T(2,128)(2,1)S(1)}, u32[]{:S(2)}, u32[]{:S(2)}) collective-permute-start(bf16[1,442992]{1,0:T(2,128)(2,1)S(1)} %collective-permute-done.7), channel_id=1, source_target_pairs={{0,1},{1,2},{2,3},{3,4},{4,5},{5,6},{6,7},{7,8},{8,9},{9,10},{10,1... | collective-permute-start | bytes 2657960 | tf_op jit(solution)/shard_map/ppermute | solution.py:268
  1673.0 37.6 %collective-permute-start.9 = (bf16[1,442992]{1,0:T(2,128)(2,1)S(1)}, bf16[1,442992]{1,0:T(2,128)(2,1)S(1)}, u32[]{:S(2)}, u32[]{:S(2)}) collective-permute-start(bf16[1,442992]{1,0:T(2,128)(2,1)S(1)} %collective-permute-done.8), channel_id=1, source_target_pairs={{0,1},{1,2},{2,3},{3,4},{4,5},{5,6},{6,7},{7,8},{8,9},{9,10},{10,1... | collective-permute-start | bytes 2657960 | tf_op jit(solution)/shard_map/ppermute | solution.py:268
  1711.8 37.6 %collective-permute-start.10 = (bf16[1,442992]{1,0:T(2,128)(2,1)S(1)}, bf16[1,442992]{1,0:T(2,128)(2,1)S(1)}, u32[]{:S(2)}, u32[]{:S(2)}) collective-permute-start(bf16[1,442992]{1,0:T(2,128)(2,1)S(1)} %collective-permute-done.9), channel_id=1, source_target_pairs={{0,1},{1,2},{2,3},{3,4},{4,5},{5,6},{6,7},{7,8},{8,9},{9,10},{10,1... | collective-permute-start | bytes 2657960 | tf_op jit(solution)/shard_map/ppermute | solution.py:268
  1750.7 37.6 %collective-permute-start.11 = (bf16[1,442992]{1,0:T(2,128)(2,1)S(1)}, bf16[1,442992]{1,0:T(2,128)(2,1)S(1)}, u32[]{:S(2)}, u32[]{:S(2)}) collective-permute-start(bf16[1,442992]{1,0:T(2,128)(2,1)S(1)} %collective-permute-done.10), channel_id=1, source_target_pairs={{0,1},{1,2},{2,3},{3,4},{4,5},{5,6},{6,7},{7,8},{8,9},{9,10},{10,1... | collective-permute-start | bytes 2657960 | tf_op jit(solution)/shard_map/ppermute | solution.py:268
  1789.5 37.6 %collective-permute-start.12 = (bf16[1,442992]{1,0:T(2,128)(2,1)S(1)}, bf16[1,442992]{1,0:T(2,128)(2,1)S(1)}, u32[]{:S(2)}, u32[]{:S(2)}) collective-permute-start(bf16[1,442992]{1,0:T(2,128)(2,1)S(1)} %collective-permute-done.11), channel_id=1, source_target_pairs={{0,1},{1,2},{2,3},{3,4},{4,5},{5,6},{6,7},{7,8},{8,9},{9,10},{10,1... | collective-permute-start | bytes 2657960 | tf_op jit(solution)/shard_map/ppermute | solution.py:268
  1828.3 38.6 %collective-permute-start.13 = (bf16[1,442992]{1,0:T(2,128)(2,1)S(1)}, bf16[1,442992]{1,0:T(2,128)(2,1)}, u32[]{:S(2)}, u32[]{:S(2)}) collective-permute-start(bf16[1,442992]{1,0:T(2,128)(2,1)S(1)} %collective-permute-done.12), channel_id=1, source_target_pairs={{0,1},{1,2},{2,3},{3,4},{4,5},{5,6},{6,7},{7,8},{8,9},{9,10},{10,1... | collective-permute-start | bytes 2657960 | tf_op jit(solution)/shard_map/ppermute | solution.py:268
  1866.9 31.9 %collective-permute-start.14 = (bf16[1,442992]{1,0:T(2,128)(2,1)}, bf16[1,442992]{1,0:T(2,128)(2,1)}, u32[]{:S(2)}, u32[]{:S(2)}) collective-permute-start(bf16[1,442992]{1,0:T(2,128)(2,1)} %collective-permute-done.13), channel_id=1, source_target_pairs={{0,1},{1,2},{2,3},{3,4},{4,5},{5,6},{6,7},{7,8},{8,9},{9,10},{10,1... | collective-permute-start | bytes 2657960 | tf_op jit(solution)/shard_map/ppermute | solution.py:268
  1878.8 20.0 copy-start.13
  1878.8 20.0 copy-start.28
  2046.4 15.6 copy-start.41
  (56 other events, 151.3 us)
Sparse Core Ops, SparseCore 0:
  508.8 734.8 all-reduce.5
  1251.4 19.8 all-reduce.3
